TPU v7x, 32 devices: a whole 2x2x4 slice. The times are simulated.
32 devices in a mesh: expert: 8 (over z, y), rep: 4 (over x, core).
Axes of the slice: x: 2, y: 2, z: 4, core: 2. Of those that a mesh axis runs over, the one named last changes fastest.
Arguments:
- tokens: bfloat16 [1024, 1024], P('expert', 'rep'), may hold values from -6 to 6
- cotangent: bfloat16 [1024, 1024], P('expert', 'rep'), may hold values from -1.796875 to 1.796875
- expert_ids: int32 [1024, 2], P('expert'), may hold values from 0 to 7, all different within a row; in each aligned block of 128 rows (0 to 127, 128 to 255, ...) at most 64 rows name the same one
- gate_values: float32 [1024, 2], P('expert'), may hold values from 0.1 to 0.9
- inner_weight: bfloat16 [8, 1024, 4096], P('expert', None, 'rep'), may hold values from -0.1875 to 0.1875
- outer_weight: bfloat16 [8, 4096, 1024], P('expert', 'rep'), may hold values from -0.09375 to 0.09375
Outputs:
- output: bfloat16 [1024, 1024], P('expert', 'rep')
- input_grads: bfloat16 [1024, 1024], P('expert', 'rep')
- gate_grads: float32 [1024, 2], P('expert')
Inputs may be any that keep to these rules, and one draw needn't show every extreme that they name: `expert_ids`: each token names 2 different experts. Among the 128 tokens of one block no expert is named more than 64 times, a bound that some block reaches.
All inputs are finite; a program needn't handle non-finite values.
Results may differ from a plain program's by a relative error of at most 0.012.
Values may be sent and summed in bfloat16 or wider, within the bound.
A program may use at most 64 MiB of HBM per device.

v0:
```python
import jax
import jax.numpy as jnp
from jax import lax
from jax.sharding import PartitionSpec as P

TOP = 2


SQRT_TWO_PI = 0.7978845608028654
CUBIC = 0.044715


def gelu_pair(preact):
    argument = SQRT_TWO_PI * (preact + CUBIC * preact * preact * preact)
    tangent = jnp.tanh(argument)
    result = 0.5 * preact * (1.0 + tangent)
    derivative = 0.5 * (1.0 + tangent) + 0.5 * preact * (1.0 - tangent * tangent) * SQRT_TWO_PI * (
        1.0 + 3.0 * CUBIC * preact * preact
    )
    return (result, derivative)


def slot_tables(expert_ids, experts, capacity):
    flat_ids = expert_ids.reshape(-1)
    matches = (flat_ids[:, None] == jnp.arange(experts, dtype=jnp.int32)[None, :]).astype(jnp.int32)
    ranked = jnp.sum((jnp.cumsum(matches, axis=0) - 1) * matches, axis=1)
    target = (flat_ids * capacity + ranked).reshape(expert_ids.shape[0], expert_ids.shape[1]).T
    slot_index = jnp.arange(experts * capacity, dtype=jnp.int32)
    return (slot_index[None, :, None] == target[:, None, :]).astype(jnp.bfloat16)


def build_slots(slot_table, gate_values, token_part, cot_part):
    slot_rows = jnp.dot(
        jnp.sum(slot_table, axis=0), token_part, preferred_element_type=jnp.float32
    ).astype(jnp.bfloat16)
    cot_float = cot_part.astype(jnp.float32)
    grad_acc = jnp.zeros((slot_table.shape[1], token_part.shape[1]), jnp.float32)
    for member in range(TOP):
        scaled = (gate_values[:, member : member + 1] * cot_float).astype(jnp.bfloat16)
        grad_acc = grad_acc + jnp.dot(
            slot_table[member], scaled, preferred_element_type=jnp.float32
        )
    return (slot_rows, grad_acc.astype(jnp.bfloat16))


def per_device(tokens, cotangent, expert_ids, gate_values, inner_weight, outer_weight):
    quarter = tokens.shape[1]
    experts = lax.axis_size("expert") * inner_weight.shape[0]
    capacity = 2 * tokens.shape[0] * TOP // experts
    slot_table = slot_tables(expert_ids, experts, capacity)
    cot_wide = cotangent.astype(jnp.float32)
    slot_rows, slot_grads = build_slots(slot_table, gate_values, tokens, cotangent)
    part_rows, part_grads = (
        lax.all_to_all(
            slot_rows.reshape(experts, capacity, quarter),
            "expert",
            split_axis=0,
            concat_axis=0,
            tiled=True,
        ),
        lax.all_to_all(
            slot_grads.reshape(experts, capacity, quarter),
            "expert",
            split_axis=0,
            concat_axis=0,
            tiled=True,
        ),
    )
    arrived_rows, arrived_grads = (
        lax.all_gather(part_rows, "rep", axis=2, tiled=True),
        lax.all_gather(part_grads, "rep", axis=2, tiled=True),
    )
    feature_width = arrived_rows.shape[2]
    expert_rows = arrived_rows.reshape(-1, feature_width)
    expert_grads = arrived_grads.reshape(-1, feature_width)
    slot_count = expert_rows.shape[0]
    inner_block = inner_weight[0]
    outer_block = outer_weight[0]
    preact = jnp.dot(expert_rows, inner_block, preferred_element_type=jnp.float32)
    result, derivative = gelu_pair(preact)
    hidden = result.astype(jnp.bfloat16)
    back_hidden = lax.dot_general(
        expert_grads, outer_block, (((1,), (1,)), ((), ())), preferred_element_type=jnp.float32
    )
    back_pre = (back_hidden * derivative).astype(jnp.bfloat16)
    term_out = lax.dot_general(
        outer_block, hidden, (((0,), (1,)), ((), ())), preferred_element_type=jnp.float32
    )
    term_in = lax.dot_general(
        inner_block, back_pre, (((1,), (1,)), ((), ())), preferred_element_type=jnp.float32
    )
    joined = jnp.concatenate([term_out, term_in], axis=1)
    summed = lax.psum_scatter(
        joined.astype(jnp.bfloat16).astype(jnp.float32).astype(jnp.bfloat16),
        "rep",
        scatter_dimension=0,
        tiled=True,
    ).astype(jnp.float32)
    expert_out = summed[:, :slot_count].T.astype(jnp.bfloat16)
    slot_input = summed[:, slot_count:].T.astype(jnp.bfloat16)
    back_out, back_input = (
        lax.all_to_all(
            expert_out.reshape(-1, capacity, quarter),
            "expert",
            split_axis=0,
            concat_axis=0,
            tiled=True,
        ),
        lax.all_to_all(
            slot_input.reshape(-1, capacity, quarter),
            "expert",
            split_axis=0,
            concat_axis=0,
            tiled=True,
        ),
    )
    back_out = back_out.reshape(-1, quarter)
    back_input = back_input.reshape(-1, quarter)
    combined = jnp.zeros((tokens.shape[0], quarter), jnp.float32)
    in_total = jnp.zeros((tokens.shape[0], quarter), jnp.float32)
    columns = []
    for member in range(TOP):
        picked = lax.dot_general(
            slot_table[member],
            back_out,
            (((0,), (0,)), ((), ())),
            preferred_element_type=jnp.float32,
        )
        combined = combined + gate_values[:, member : member + 1] * picked
        columns.append(jnp.sum(cot_wide * picked, axis=1))
        in_total = in_total + lax.dot_general(
            slot_table[member],
            back_input,
            (((0,), (0,)), ((), ())),
            preferred_element_type=jnp.float32,
        )
    output = combined.astype(jnp.bfloat16)
    input_grads = in_total.astype(jnp.bfloat16)
    gate_grads = lax.psum(jnp.stack(columns, axis=1), "rep")
    return (output, input_grads, gate_grads)


def solution(mesh):
    placed = (
        P("expert", "rep"),
        P("expert", "rep"),
        P("expert", None),
        P("expert", None),
        P("expert", None, "rep"),
        P("expert", "rep", None),
    )
    return jax.shard_map(
        per_device,
        mesh=mesh,
        in_specs=placed,
        out_specs=(P("expert", "rep"), P("expert", "rep"), P("expert", None)),
        check_vma=False,
    )
```

profile of v0, /device:TPU:0, one launch (start us, length us, event | category | flops | bytes accessed | tf_op | source)
XLA Modules:
  0.0 145.1 jit_solution(12485271527815582667)
XLA Ops:
  7.2 0.9 copy.19
  8.2 0.1 eq.43
  8.3 0.1 eq.39
  8.5 0.6 reduce-window.6
  9.0 0.2 slice_reduce_fusion
  9.3 0.1 fusion.49
  9.4 0.1 reduce_sum.42
  9.6 0.7 add_bitcast_fusion
  10.4 1.1 convolution_convert_fusion
  11.4 16.1 %all_to_all.20 = bf16[8,64,256]{2,1,0:T(8,128)(2,1)} all-to-all(bf16[8,64,256]{2,1,0:T(8,128)(2,1)S(1)} %bitcast.77), channel_id=1, replica_groups=mesh['expert'=8,'rep'=4] {'expert'}, dimensions={0} | all-to-all | bytes 524288 | tf_op jit(solution)/shard_map/all_to_all | solution.py:54
  27.6 0.8 slice_bitcast_fusion.8
  28.4 0.1 iota_compare_fusion
  28.4 1.1 fusion.39
  29.6 0.3 fusion.29
  29.9 12.1 %all_to_all.21 = bf16[8,64,256]{2,1,0:T(8,128)(2,1)} all-to-all(bf16[8,64,256]{2,1,0:T(8,128)(2,1)S(1)} %bitcast.74), channel_id=1, replica_groups=mesh['expert'=8,'rep'=4] {'expert'}, dimensions={0} | all-to-all | bytes 524288 | tf_op jit(solution)/shard_map/all_to_all | solution.py:61
  42.0 1.5 %all-gather.3.cloned.1.call-done = bf16[8,64,1024]{2,1,0:T(8,128)(2,1)} async-done(((bf16[8,64,256]{2,1,0:T(8,128)(2,1)}), bf16[8,64,1024]{2,1,0:T(8,128)(2,1)}) %all-gather.3.cloned.1.call-update) | async-done | bytes 1048592 | tf_op jit(solution)/shard_map/all_gather | solution.py:70
  43.6 2.6 %fusion.13 = f32[512,1024]{1,0:T(8,128)S(1)} fusion(bf16[512,1024]{1,0:T(8,128)(2,1)} %bitcast.81, bf16[1,1024,1024]{2,1,0:T(8,128)(2,1)S(1)} %copy-done), kind=kOutput, calls=%fused_computation.16 | convolution fusion | flops 1073741824 | bytes 5242880 | tf_op jit(solution)/shard_map/dot_general | solution.py:79
  46.2 1.3 copy-done.3
  47.5 1.4 fusion.21
  49.0 13.0 %all-gather.5.cloned.1.call-done = bf16[8,64,1024]{2,1,0:T(8,128)(2,1)} async-done(((bf16[8,64,256]{2,1,0:T(8,128)(2,1)}), bf16[8,64,1024]{2,1,0:T(8,128)(2,1)}) %all-gather.5.cloned.1.call-update) | async-done | bytes 1048592 | tf_op jit(solution)/shard_map/all_gather | solution.py:71
  62.0 6.2 %fusion.24 = bf16[1024,512]{0,1:T(8,128)(2,1)} fusion(bf16[1,1024,1024]{2,1,0:T(8,128)(2,1)S(1)} %copy-done, f32[512,1024]{1,0:T(8,128)} %copy-done.3, bf16[512,1024]{1,0:T(8,128)(2,1)} %bitcast.82, bf16[1,1024,1024]{2,1,0:T(8,128)(2,1)} %param.11), kind=kOutput, calls=%fused_computation.22 | convolution fusion | flops 2157969408 | bytes 8388608 | tf_op jit(solution)/shard_map/dot_general | solution.py:89
  68.2 2.8 %pad_maximum_fusion = bf16[1024,1024]{0,1:T(8,128)(2,1)} fusion(bf16[1024,512]{0,1:T(8,128)(2,1)} %fusion.24, bf16[1024,512]{0,1:T(8,128)(2,1)S(1)} %fusion.21), kind=kLoop, calls=%fused_computation.9 | loop fusion | flops 4194304 | bytes 4194304 | tf_op jit(solution)/shard_map/concatenate | solution.py:92
  71.1 31.6 %reduce-scatter.2.cloned.1.call-done = bf16[256,1024]{0,1:T(8,128)(2,1)} async-done(((bf16[1024,1024]{0,1:T(8,128)(2,1)}), bf16[256,1024]{0,1:T(8,128)(2,1)}) %reduce-scatter.2.cloned.1.call-update) | async-done | bytes 524304 | tf_op jit(solution)/shard_map/reduce_scatter | solution.py:93
  102.7 1.8 %fusion.60 = (bf16[256,512]{0,1:T(8,128)(2,1)S(1)}, bf16[256,512]{0,1:T(8,128)(2,1)}) fusion(bf16[256,1024]{0,1:T(8,128)(2,1)} %reduce-scatter.2.cloned.1.call-done), kind=kLoop, calls=%fused_computation.70 | loop fusion | bytes 1048576 | tf_op jit(solution)/shard_map/slice | solution.py:100
  104.4 14.2 %all_to_all.22 = bf16[8,64,256]{2,1,0:T(8,128)(2,1)S(1)} all-to-all(bf16[8,64,256]{2,1,0:T(8,128)(2,1)S(1)} %bitcast.78), channel_id=1, replica_groups=mesh['expert'=8,'rep'=4] {'expert'}, dimensions={0} | all-to-all | bytes 524288 | tf_op jit(solution)/shard_map/all_to_all | solution.py:109
  118.7 3.6 %all-to-all-start.2 = ((bf16[8,64,256]{2,1,0:T(8,128)(2,1)}), bf16[8,64,256]{2,1,0:T(8,128)(2,1)S(1)}, u32[]{:S(2)}, u32[]{:S(2)}) async-start(bf16[8,64,256]{2,1,0:T(8,128)(2,1)} %bitcast.16), calls=%async_computation.3 | async-start | bytes 524288 | tf_op jit(solution)/shard_map/all_to_all | solution.py:102
  122.2 0.3 fusion.37
  122.5 0.9 fusion.30
  123.4 7.4 %all-to-all-done.2 = bf16[8,64,256]{2,1,0:T(8,128)(2,1)S(1)} async-done(((bf16[8,64,256]{2,1,0:T(8,128)(2,1)}), bf16[8,64,256]{2,1,0:T(8,128)(2,1)S(1)}, u32[]{:S(2)}, u32[]{:S(2)}) %all-to-all-start.2) | async-done | bytes 262176 | tf_op jit(solution)/shard_map/all_to_all | solution.py:102
  130.8 0.3 fusion.40
  131.1 1.0 fusion.43
  132.1 6.5 %psum.7 = f32[128,2]{0,1:T(2,128)} all-reduce(f32[128,2]{0,1:T(2,128)S(1)} %pad_maximum_fusion.1), channel_id=1, replica_groups=mesh['expert'=8,'rep'=4] {'rep'}, use_global_device_ids=true, to_apply=%region_7.8 | all-reduce | flops 256 | bytes 2048 | tf_op jit(solution)/shard_map/psum | solution.py:139
  (19 shorter events, 0.4 us)
Async XLA Ops:
  7.2 36.4 %copy-start = (bf16[1,1024,1024]{2,1,0:T(8,128)(2,1)S(1)}, bf16[1,1024,1024]{2,1,0:T(8,128)(2,1)}, u32[]{:S(2)}) copy-start(bf16[1,1024,1024]{2,1,0:T(8,128)(2,1)} %param.10) | copy-start | bytes 6291460
  7.2 22.4 %copy-start.1 = (bf16[128,256]{1,0:T(8,128)(2,1)S(1)}, bf16[128,256]{1,0:T(8,128)(2,1)}, u32[]{:S(2)}) copy-start(bf16[128,256]{1,0:T(8,128)(2,1)} %param.7) | copy-start | bytes 196612
  7.2 36.4 %all-gather.3.cloned.1.call-start = ((), (), s32[]{:S(2)}) async-start(), calls=%async_computation.5 | async-start | bytes 1310720 | tf_op jit(solution)/shard_map/all_gather | solution.py:70
  27.6 34.4 %all-gather.5.cloned.1.call-start = ((), (), s32[]{:S(2)}) async-start(), calls=%async_computation.6 | async-start | bytes 1310720 | tf_op jit(solution)/shard_map/all_gather | solution.py:71
  42.0 60.7 %reduce-scatter.2.cloned.1.call-start = ((), (), s32[]{:S(2)}) async-start(), calls=%async_computation.7 | async-start | bytes 2621440 | tf_op jit(solution)/shard_map/reduce_scatter | solution.py:93
  43.6 4.0 %copy-start.2 = (bf16[1,1024,1024]{2,1,0:T(8,128)(2,1)S(1)}, bf16[1,1024,1024]{2,1,0:T(8,128)(2,1)}, u32[]{:S(2)}) copy-start(bf16[1,1024,1024]{2,1,0:T(8,128)(2,1)} %param.11) | copy-start | bytes 6291460
  46.2 1.4 copy-start.3
  118.7 12.2 %all-to-all-start.2 = ((bf16[8,64,256]{2,1,0:T(8,128)(2,1)}), bf16[8,64,256]{2,1,0:T(8,128)(2,1)S(1)}, u32[]{:S(2)}, u32[]{:S(2)}) async-start(bf16[8,64,256]{2,1,0:T(8,128)(2,1)} %bitcast.16), calls=%async_computation.3 | async-start | bytes 524288 | tf_op jit(solution)/shard_map/all_to_all | solution.py:102
Sparse Core Ops, SparseCore 0:
  27.7 15.8 all-gather.2
  45.1 16.8 all-gather.4
  71.2 31.4 reduce-scatter.1
where the time goes:
time: 146 us; the launch traced here: 145 us
  waiting for transfers between devices  53.6 us (37%)
  blocking collectives  48.9 us (33%)
  matrix products  15.2 us (10%)
  between operations  13.8 us (9%)
  local copies, waits for them, and re-layouts  5.5 us (4%)
  other arithmetic  4.43 us (3%)
  starting transfers between devices  3.71 us (3%)
    reduce_scatter x1, waiting for transfers between devices, per_device(): lax.psum_scatter(joined.astype(jnp.bfloat16).astype(jnp.float32).astype(j...  31.6 us
    all_to_all x1, blocking collectives, per_device(): lax.all_to_all(slot_rows.reshape(experts, capacity, quarter), 'expert', s...  16.1 us
    all_to_all x1, blocking collectives, per_device(): lax.all_to_all(slot_input.reshape(-1, capacity, quarter), 'expert', split...  14.2 us
    all_gather x1, waiting for transfers between devices, per_device(): lax.all_gather(part_grads, 'rep', axis=2, tiled=True)  13 us
    all_to_all x1, blocking collectives, per_device(): lax.all_to_all(slot_grads.reshape(experts, capacity, quarter), 'expert',...  12.1 us
    all_to_all x1, waiting for transfers between devices, per_device(): lax.all_to_all(expert_out.reshape(-1, capacity, quarter), 'expert', split...  7.39 us
    psum x1, blocking collectives, per_device(): gate_grads = lax.psum(jnp.stack(columns, axis=1), 'rep')  6.48 us
    dot_general x1, matrix products, per_device(): lax.dot_general(inner_block, back_pre, (((1,), (1,)), ((), ())), preferre...  6.23 us
  transfers between devices with their start and end apart: 4, of which 4 were waited for; matrix products, arithmetic and copies ran while one was open for 5% of the time, Pallas kernels for 0%

commit v1 on v0

--- a/solution.py
+++ b/solution.py
@@ -1,6 +1,8 @@
 import jax
 import jax.numpy as jnp
 from jax import lax
+from jax.experimental import pallas as pl
+from jax.experimental.pallas import tpu as pltpu
 from jax.sharding import PartitionSpec as P
 
 TOP = 2
@@ -22,8 +24,11 @@
 
 def slot_tables(expert_ids, experts, capacity):
     flat_ids = expert_ids.reshape(-1)
-    matches = (flat_ids[:, None] == jnp.arange(experts, dtype=jnp.int32)[None, :]).astype(jnp.int32)
-    ranked = jnp.sum((jnp.cumsum(matches, axis=0) - 1) * matches, axis=1)
+    matches = (flat_ids[:, None] == jnp.arange(experts, dtype=jnp.int32)[None, :]).astype(jnp.bfloat16)
+    order = jnp.arange(flat_ids.shape[0], dtype=jnp.int32)
+    earlier = (order[None, :] < order[:, None]).astype(jnp.bfloat16)
+    counts = jnp.dot(earlier, matches, preferred_element_type=jnp.float32)
+    ranked = jnp.sum(counts * matches.astype(jnp.float32), axis=1).astype(jnp.int32)
     target = (flat_ids * capacity + ranked).reshape(expert_ids.shape[0], expert_ids.shape[1]).T
     slot_index = jnp.arange(experts * capacity, dtype=jnp.int32)
     return (slot_index[None, :, None] == target[:, None, :]).astype(jnp.bfloat16)
@@ -43,7 +48,7 @@
     return (slot_rows, grad_acc.astype(jnp.bfloat16))
 
 
-def per_device(tokens, cotangent, expert_ids, gate_values, inner_weight, outer_weight):
+def per_device_xla(tokens, cotangent, expert_ids, gate_values, inner_weight, outer_weight):
     quarter = tokens.shape[1]
     experts = lax.axis_size("expert") * inner_weight.shape[0]
     capacity = 2 * tokens.shape[0] * TOP // experts
@@ -140,6 +145,291 @@
     return (output, input_grads, gate_grads)
 
 
+MESH = pl.DeviceIdType.MESH
+GROUP = 2
+
+
+def flip(index, bits):
+    step = 1
+    result = index
+    while step <= bits:
+        if bits & step:
+            result = result + step * (1 - 2 * lax.rem(lax.div(index, step), 2))
+        step *= 2
+    return result
+
+
+def kernel(
+    ids, gates, tokens, cotangent, inner_any, outer_any,
+    output, input_grads, gate_grads,
+    inner, outer, sent, arrived, square, hidden, back_pre, own,
+    core_out, core_in, chip_out, chip_in, back_sent, back_in, gate_out, gate_in,
+    weight_sem, a2a_send, a2a_recv, gather_send, gather_recv, core_send, core_recv,
+    chip_send, chip_recv, back_send, back_recv, gate_send, gate_recv,
+):
+    experts, _, capacity, quarter = sent.shape
+    rows = tokens.shape[0]
+    reps = arrived.shape[0]
+    units = outer.shape[0]
+    chunks = experts // GROUP
+    span = GROUP * capacity
+    me, part = lax.axis_index("expert"), lax.axis_index("rep")
+
+    def to_expert(j):
+        return (flip(me, j), part)
+
+    def to_rep(q):
+        return (me, flip(part, q))
+
+    barrier = pltpu.get_barrier_semaphore()
+    for j in range(1, experts):
+        pl.semaphore_signal(barrier, inc=1, device_id=to_expert(j), device_id_type=MESH)
+    for q in range(1, reps):
+        pl.semaphore_signal(barrier, inc=1, device_id=to_rep(q), device_id_type=MESH)
+
+    loads = []
+    for q in range(reps):
+        start = pl.multiple_of(flip(part, q) * quarter, quarter)
+        here = pl.ds(q * quarter, quarter)
+        loads.append(pltpu.make_async_copy(inner_any.at[pl.ds(start, quarter), :], inner.at[here, :], weight_sem.at[0, q]))
+        loads.append(pltpu.make_async_copy(outer_any.at[:, pl.ds(start, quarter)], outer.at[:, here], weight_sem.at[1, q]))
+    for load in loads:
+        load.start()
+
+    padded = max(experts, 16)
+    expert_iota = lax.broadcasted_iota(jnp.int32, (padded, rows), 0)
+    match = [jnp.where(expert_iota == ids[k : k + 1, :], 1.0, 0.0) for k in range(TOP)]
+    before = lax.broadcasted_iota(jnp.int32, (rows, rows), 0) < lax.broadcasted_iota(jnp.int32, (rows, rows), 1)
+    prior = jnp.dot(
+        (match[0] + match[1]).astype(jnp.bfloat16),
+        jnp.where(before, 1.0, 0.0).astype(jnp.bfloat16),
+        preferred_element_type=jnp.float32,
+    )
+    targets = []
+    for k in range(TOP):
+        rank = jnp.sum(prior * match[k], axis=0, keepdims=True).astype(jnp.int32)
+        targets.append((ids[k : k + 1, :] ^ me) * capacity + rank)
+    slot_iota = lax.broadcasted_iota(jnp.int32, (experts * capacity, rows), 0)
+    table = [jnp.where(slot_iota == targets[k], 1.0, 0.0).astype(jnp.bfloat16) for k in range(TOP)]
+    square[...] = jnp.zeros_like(square)
+    for k in range(TOP):
+        square[k : k + 1, :] = targets[k].astype(jnp.float32)
+        square[TOP + k : TOP + k + 1, :] = gates[k : k + 1, :]
+    columns = square[...].T
+    gate_columns = [columns[:, TOP + k : TOP + k + 1] for k in range(TOP)]
+    cot = cotangent[...].astype(jnp.float32)
+    slot_rows = jnp.dot(table[0] + table[1], tokens[...], preferred_element_type=jnp.float32).astype(jnp.bfloat16)
+    slot_grads = jnp.dot(
+        table[0], (gate_columns[0] * cot).astype(jnp.bfloat16), preferred_element_type=jnp.float32
+    ) + jnp.dot(table[1], (gate_columns[1] * cot).astype(jnp.bfloat16), preferred_element_type=jnp.float32)
+    slot_grads = slot_grads.astype(jnp.bfloat16)
+    for j in range(experts):
+        target = arrived.at[0, 0] if j == 0 else sent.at[j]
+        target[0] = slot_rows[j * capacity : (j + 1) * capacity, :]
+        target[1] = slot_grads[j * capacity : (j + 1) * capacity, :]
+
+    def remote(source, target, send, recv, device):
+        return pltpu.make_async_remote_copy(
+            src_ref=source, dst_ref=target, send_sem=send, recv_sem=recv, device_id=device, device_id_type=MESH
+        )
+
+    dispatch = {
+        j: remote(sent.at[j], arrived.at[0, j], a2a_send.at[j], a2a_recv.at[j], to_expert(j))
+        for j in range(1, experts)
+    }
+    gather = {
+        (g, j): remote(arrived.at[a, j], arrived.at[b, j], gather_send.at[g, j], gather_recv.at[g, j], to_rep(hop))
+        for g, (a, b, hop) in enumerate(((0, 1, 1), (0, 2, 2), (2, 3, 1)))
+        for j in range(experts)
+    }
+    core = [remote(core_out.at[c], core_in.at[c], core_send.at[c], core_recv.at[c], to_rep(1)) for c in range(chunks)]
+    chip = [remote(chip_out.at[c], chip_in.at[c], chip_send.at[c], chip_recv.at[c], to_rep(2)) for c in range(chunks)]
+    back = {
+        j: remote(back_sent.at[j], back_in.at[j], back_send.at[j], back_recv.at[j], to_expert(j))
+        for j in range(1, experts)
+    }
+    gate = [remote(gate_out, gate_in.at[q], gate_send.at[q], gate_recv.at[q], to_rep(q)) for q in range(1, reps)]
+
+    pl.semaphore_wait(barrier, experts - 1 + reps - 1)
+
+    def members(c):
+        return range(c * GROUP, (c + 1) * GROUP)
+
+    def step_a(c):
+        for j in members(c):
+            if j:
+                dispatch[j].wait_recv()
+            gather[1, j].start()
+            gather[0, j].start()
+
+    def step_b(c):
+        for j in members(c):
+            gather[1, j].wait_recv()
+            gather[2, j].start()
+
+    def step_c(c):
+        for j in members(c):
+            gather[0, j].wait_recv()
+            gather[2, j].wait_recv()
+        if c == 0:
+            for load in loads:
+                load.wait()
+
+        def operand(kind):
+            return jnp.concatenate(
+                [jnp.concatenate([arrived[q, j, kind] for q in range(reps)], axis=1) for j in members(c)], axis=0
+            )
+
+        expert_rows, expert_grads = operand(0), operand(1)
+        tile = min(units, 256)
+        for h in range(units // tile):
+            at = slice(h * tile, (h + 1) * tile)
+            preact = jnp.dot(expert_rows, inner[:, at], preferred_element_type=jnp.float32)
+            spread = lax.dot_general(
+                expert_grads, outer[at, :], (((1,), (1,)), ((), ())), preferred_element_type=jnp.float32
+            )
+            result, derivative = gelu_pair(preact)
+            hidden[:, at] = result.astype(jnp.bfloat16)
+            back_pre[:, at] = (spread * derivative).astype(jnp.bfloat16)
+        for q in (1, 3, 0, 2):
+            at = slice(q * quarter, (q + 1) * quarter)
+            term_out = jnp.dot(hidden[...], outer[:, at], preferred_element_type=jnp.float32)
+            term_in = lax.dot_general(
+                back_pre[...], inner[at, :], (((1,), (1,)), ((), ())), preferred_element_type=jnp.float32
+            )
+            if q % 2:
+                core_out[c, q // 2, 0] = term_out.astype(jnp.bfloat16)
+                core_out[c, q // 2, 1] = term_in.astype(jnp.bfloat16)
+                if q == 3:
+                    core[c].start()
+            else:
+                own[c, q // 2, 0] = term_out
+                own[c, q // 2, 1] = term_in
+
+    def step_d(c):
+        core[c].wait_recv()
+        chip_out[c] = (own[c, 1] + core_in[c, 1].astype(jnp.float32)).astype(jnp.bfloat16)
+        chip[c].start()
+        own[c, 0] = own[c, 0] + core_in[c, 0].astype(jnp.float32)
+
+    def step_e(c):
+        chip[c].wait_recv()
+        total = (own[c, 0] + chip_in[c].astype(jnp.float32)).astype(jnp.bfloat16)
+        for i, j in enumerate(members(c)):
+            target = back_sent.at[j] if j else back_in.at[0]
+            target[...] = total[:, i * capacity : (i + 1) * capacity, :]
+            if j:
+                back[j].start()
+
+    for j in send_order(experts):
+        dispatch[j].start()
+    steps = dict(a=step_a, b=step_b, c=step_c, d=step_d, e=step_e)
+    for name, c in schedule(chunks):
+        steps[name](c)
+
+    lane_iota = lax.broadcasted_iota(jnp.int32, (rows, span), 1).astype(jnp.float32)
+    picked = [jnp.zeros((rows, quarter), jnp.float32) for _ in range(TOP)]
+    in_total = jnp.zeros((rows, quarter), jnp.float32)
+    for c in range(chunks):
+        for j in members(c):
+            if j:
+                back[j].wait_recv()
+        slots = [
+            jnp.where(lane_iota + float(c * span) == columns[:, k : k + 1], 1.0, 0.0).astype(jnp.bfloat16)
+            for k in range(TOP)
+        ]
+        outs, ins = (jnp.concatenate([back_in[j, kind] for j in members(c)], axis=0) for kind in range(2))
+        for k in range(TOP):
+            picked[k] = picked[k] + jnp.dot(slots[k], outs, preferred_element_type=jnp.float32)
+        in_total = in_total + jnp.dot(slots[0] + slots[1], ins, preferred_element_type=jnp.float32)
+    lane = lax.broadcasted_iota(jnp.int32, (rows, square.shape[1]), 1)
+    sums = jnp.zeros(square.shape, jnp.float32)
+    for k in range(TOP):
+        sums = jnp.where(lane == k, jnp.sum(cot * picked[k], axis=1, keepdims=True), sums)
+    gate_out[...] = sums.T[: gate_out.shape[0], :]
+    for copy in gate:
+        copy.start()
+    output[...] = (gate_columns[0] * picked[0] + gate_columns[1] * picked[1]).astype(jnp.bfloat16)
+    input_grads[...] = in_total.astype(jnp.bfloat16)
+    for copy in (*dispatch.values(), *gather.values(), *core, *chip, *back.values()):
+        copy.wait_send()
+    for copy in gate:
+        copy.wait()
+    total = (gate_out[...] + gate_in[1]) + (gate_in[2] + gate_in[3])
+    gate_grads[...] = total[:TOP, :]
+
+
+def send_order(experts):
+    half = experts // 2
+    near, far = list(range(1, half)), list(range(half, experts))
+    order = []
+    while near or far:
+        if near:
+            order.append(near.pop(0))
+        if far:
+            order.append(far.pop(0))
+    return order
+
+
+def schedule(chunks):
+    plan = []
+    for s in range(chunks + 4):
+        for name, lag in (("a", 0), ("b", 1), ("e", 4), ("d", 3), ("c", 2)):
+            if 0 <= s - lag < chunks:
+                plan.append((name, s - lag))
+    return plan
+
+
+def per_device(tokens, cotangent, expert_ids, gate_values, inner_weight, outer_weight):
+    rows, quarter = tokens.shape
+    experts, reps = lax.axis_size("expert"), lax.axis_size("rep")
+    capacity = 2 * rows * TOP // experts
+    width, units = inner_weight.shape[1:]
+    fits = (
+        inner_weight.shape[0] == 1 and reps == 4 and capacity % 16 == 0 and rows % 128 == 0 and quarter % 128 == 0
+        and units % 256 == 0 and experts & (experts - 1) == 0 and experts % GROUP == 0
+    )
+    if not fits:
+        return per_device_xla(tokens, cotangent, expert_ids, gate_values, inner_weight, outer_weight)
+    chunks, span = experts // GROUP, GROUP * capacity
+    half, dma = jnp.bfloat16, pltpu.SemaphoreType.DMA
+    output, input_grads, gate_grads = pl.pallas_call(
+        kernel,
+        out_shape=(
+            jax.ShapeDtypeStruct((rows, quarter), half),
+            jax.ShapeDtypeStruct((rows, quarter), half),
+            jax.ShapeDtypeStruct((TOP, rows), jnp.float32),
+        ),
+        in_specs=[pl.BlockSpec(memory_space=pltpu.VMEM)] * 4 + [pl.BlockSpec(memory_space=pl.ANY)] * 2,
+        out_specs=[pl.BlockSpec(memory_space=pltpu.VMEM)] * 3,
+        scratch_shapes=[
+            pltpu.VMEM((width, units), half),
+            pltpu.VMEM((units, width), half),
+            pltpu.VMEM((experts, 2, capacity, quarter), half),
+            pltpu.VMEM((reps, experts, 2, capacity, quarter), half),
+            pltpu.VMEM((rows, rows), jnp.float32),
+            pltpu.VMEM((span, units), half),
+            pltpu.VMEM((span, units), half),
+            pltpu.VMEM((chunks, 2, 2, span, quarter), jnp.float32),
+            pltpu.VMEM((chunks, 2, 2, span, quarter), half),
+            pltpu.VMEM((chunks, 2, 2, span, quarter), half),
+            pltpu.VMEM((chunks, 2, span, quarter), half),
+            pltpu.VMEM((chunks, 2, span, quarter), half),
+            pltpu.VMEM((experts, 2, capacity, quarter), half),
+            pltpu.VMEM((experts, 2, capacity, quarter), half),
+            pltpu.VMEM((8, rows), jnp.float32),
+            pltpu.VMEM((reps, 8, rows), jnp.float32),
+            dma((2, reps)), dma((experts,)), dma((experts,)), dma((3, experts)), dma((3, experts)),
+            dma((chunks,)), dma((chunks,)), dma((chunks,)), dma((chunks,)),
+            dma((experts,)), dma((experts,)), dma((reps,)), dma((reps,)),
+        ],
+        compiler_params=pltpu.CompilerParams(
+            collective_id=0, has_side_effects=True, vmem_limit_bytes=56 * 2**20
+        ),
+    )(expert_ids.T, gate_values.T, tokens, cotangent, inner_weight[0], outer_weight[0])
+    return (output, input_grads, gate_grads.T)
+
+
 def solution(mesh):
     placed = (
         P("expert", "rep"),

time: 146 us -> 56.3 us (0.39)
  waiting for transfers between devices: 53.6 us -> 0 us
  Pallas kernels: 0 us -> 51.2 us
  blocking collectives: 48.9 us -> 0 us
  matrix products: 15.2 us -> 0 us
  between operations: 13.8 us -> 0.64 us
  other arithmetic: 4.43 us -> 0 us
  starting transfers between devices: 3.71 us -> 0 us
    pallas_call x0 -> x1, Pallas kernels: none -> 51.2 us  [per_device(): pl.pallas_call(kernel, out_shape=(jax.ShapeDtypeStruct((rows, quarter), h...]
    all_to_all x3 -> x0, blocking collectives: 42.4 us -> none  [the longest x1 16.1 us: per_device(): lax.all_to_all(slot_rows.reshape(experts, capacity, quarter), 'expert', s...]
    reduce_scatter x1 -> x0, waiting for transfers between devices: 31.6 us -> none  [per_device(): lax.psum_scatter(joined.astype(jnp.bfloat16).astype(jnp.float32).astype(j...]
    dot_general x10 -> x0, matrix products: 15.2 us -> none  [the longest x1 6.23 us: per_device(): lax.dot_general(inner_block, back_pre, (((1,), (1,)), ((), ())), preferre...]
    all_gather x2 -> x0, waiting for transfers between devices: 14.6 us -> none  [the longest x1 13 us: per_device(): lax.all_gather(part_grads, 'rep', axis=2, tiled=True)]
    all_to_all x1 -> x0, waiting for transfers between devices: 7.39 us -> none  [per_device(): lax.all_to_all(expert_out.reshape(-1, capacity, quarter), 'expert', split...]
    psum x1 -> x0, blocking collectives: 6.48 us -> none  [per_device(): gate_grads = lax.psum(jnp.stack(columns, axis=1), 'rep')]
    all_to_all x1 -> x0, starting transfers between devices: 3.59 us -> none  [per_device(): lax.all_to_all(expert_out.reshape(-1, capacity, quarter), 'expert', split...]
  transfers between devices with their start and end apart: 4 -> 0, of which waited for: 4 -> 0; matrix products, arithmetic and copies ran while one was open for 5% -> 0% of each run, Pallas kernels for 0% -> 0%
where the time goes in v1:
time: 56.3 us; the launch traced here: 56 us
  Pallas kernels  51.2 us (91%)
  local copies, waits for them, and re-layouts  4.17 us (7%)
  between operations  0.64 us (1%)
    pallas_call x1, Pallas kernels, per_device(): pl.pallas_call(kernel, out_shape=(jax.ShapeDtypeStruct((rows, quarter), h...  51.2 us
    unnamed x3, local copies, waits for them, and re-layouts  4.17 us

profile of v1, /device:TPU:0, one launch (start us, length us, event | category | flops | bytes accessed | tf_op | source)
XLA Modules:
  0.0 56.0 jit_solution(12387843323151930461)
XLA Ops:
  0.6 51.2 %shard_map.85 = (bf16[128,256]{1,0:T(8,128)(2,1)}, bf16[128,256]{1,0:T(8,128)(2,1)}, f32[2,128]{1,0:T(2,128)}) custom-call(s32[2,128]{1,0:T(2,128)} %bitcast.8, f32[2,128]{1,0:T(2,128)} %bitcast.9, bf16[128,256]{1,0:T(8,128)(2,1)} %tokens.1, bf16[128,256]{1,0:T(8,128)(2,1)} %cotangent.1, bf16[1024,1024]{1,0:T(8,128)(2,1)} %bitcast.5, bf16[1024,1024]{1,0:T(8,128)(2,1)} %bitcast.6), custom_call_target="tpu_custom_call" | custom-call | tf_op jit(solution)/shard_map/pallas_call | solution.py:396
  51.8 1.5 %copy.12 = bf16[128,256]{1,0:T(8,128)(2,1)} copy(bf16[128,256]{1,0:T(8,128)(2,1)} %get-tuple-element.12) | data formatting | bytes 131072
  53.3 1.5 %copy.13 = bf16[128,256]{1,0:T(8,128)(2,1)} copy(bf16[128,256]{1,0:T(8,128)(2,1)} %get-tuple-element.13) | data formatting | bytes 131072
  54.8 1.2 %copy.14 = f32[128,2]{0,1:T(2,128)} copy(f32[128,2]{0,1:T(2,128)} %bitcast.7) | data formatting | bytes 2048

commit v2 on v1

--- a/solution.py
+++ b/solution.py
@@ -242,7 +242,11 @@
         for g, (a, b, hop) in enumerate(((0, 1, 1), (0, 2, 2), (2, 3, 1)))
         for j in range(experts)
     }
-    core = [remote(core_out.at[c], core_in.at[c], core_send.at[c], core_recv.at[c], to_rep(1)) for c in range(chunks)]
+    core = {
+        (c, i): remote(core_out.at[c, i], core_in.at[c, i], core_send.at[c, i], core_recv.at[c, i], to_rep(1))
+        for c in range(chunks)
+        for i in range(2)
+    }
     chip = [remote(chip_out.at[c], chip_in.at[c], chip_send.at[c], chip_recv.at[c], to_rep(2)) for c in range(chunks)]
     back = {
         j: remote(back_sent.at[j], back_in.at[j], back_send.at[j], back_recv.at[j], to_expert(j))
@@ -271,7 +275,7 @@
         for j in members(c):
             gather[0, j].wait_recv()
             gather[2, j].wait_recv()
-        if c == 0:
+        if c == chunk_order(chunks)[0]:
             for load in loads:
                 load.wait()
 
@@ -291,7 +295,9 @@
             result, derivative = gelu_pair(preact)
             hidden[:, at] = result.astype(jnp.bfloat16)
             back_pre[:, at] = (spread * derivative).astype(jnp.bfloat16)
-        for q in (1, 3, 0, 2):
+
+    def step_o(c):
+        for q in (3, 2, 1, 0):
             at = slice(q * quarter, (q + 1) * quarter)
             term_out = jnp.dot(hidden[...], outer[:, at], preferred_element_type=jnp.float32)
             term_in = lax.dot_general(
@@ -300,21 +306,20 @@
             if q % 2:
                 core_out[c, q // 2, 0] = term_out.astype(jnp.bfloat16)
                 core_out[c, q // 2, 1] = term_in.astype(jnp.bfloat16)
-                if q == 3:
-                    core[c].start()
+                core[c, q // 2].start()
             else:
                 own[c, q // 2, 0] = term_out
                 own[c, q // 2, 1] = term_in
 
     def step_d(c):
-        core[c].wait_recv()
+        core[c, 1].wait_recv()
         chip_out[c] = (own[c, 1] + core_in[c, 1].astype(jnp.float32)).astype(jnp.bfloat16)
         chip[c].start()
-        own[c, 0] = own[c, 0] + core_in[c, 0].astype(jnp.float32)
 
     def step_e(c):
+        core[c, 0].wait_recv()
         chip[c].wait_recv()
-        total = (own[c, 0] + chip_in[c].astype(jnp.float32)).astype(jnp.bfloat16)
+        total = (own[c, 0] + core_in[c, 0].astype(jnp.float32) + chip_in[c].astype(jnp.float32)).astype(jnp.bfloat16)
         for i, j in enumerate(members(c)):
             target = back_sent.at[j] if j else back_in.at[0]
             target[...] = total[:, i * capacity : (i + 1) * capacity, :]
@@ -323,14 +328,14 @@
 
     for j in send_order(experts):
         dispatch[j].start()
-    steps = dict(a=step_a, b=step_b, c=step_c, d=step_d, e=step_e)
+    steps = dict(a=step_a, b=step_b, c=step_c, o=step_o, d=step_d, e=step_e)
     for name, c in schedule(chunks):
         steps[name](c)
 
     lane_iota = lax.broadcasted_iota(jnp.int32, (rows, span), 1).astype(jnp.float32)
     picked = [jnp.zeros((rows, quarter), jnp.float32) for _ in range(TOP)]
     in_total = jnp.zeros((rows, quarter), jnp.float32)
-    for c in range(chunks):
+    for c in chunk_order(chunks):
         for j in members(c):
             if j:
                 back[j].wait_recv()
@@ -351,7 +356,7 @@
         copy.start()
     output[...] = (gate_columns[0] * picked[0] + gate_columns[1] * picked[1]).astype(jnp.bfloat16)
     input_grads[...] = in_total.astype(jnp.bfloat16)
-    for copy in (*dispatch.values(), *gather.values(), *core, *chip, *back.values()):
+    for copy in (*dispatch.values(), *gather.values(), *core.values(), *chip, *back.values()):
         copy.wait_send()
     for copy in gate:
         copy.wait()
@@ -371,12 +376,17 @@
     return order
 
 
+def chunk_order(chunks):
+    near, far = list(range(chunks // 2)), list(range(chunks // 2, chunks))
+    return near[:1] + far + near[1:]
+
+
 def schedule(chunks):
     plan = []
     for s in range(chunks + 4):
-        for name, lag in (("a", 0), ("b", 1), ("e", 4), ("d", 3), ("c", 2)):
+        for name, lag in (("a", 0), ("c", 2), ("b", 1), ("e", 4), ("d", 3), ("o", 2)):
             if 0 <= s - lag < chunks:
-                plan.append((name, s - lag))
+                plan.append((name, chunk_order(chunks)[s - lag]))
     return plan
 
 
@@ -420,7 +430,7 @@
             pltpu.VMEM((8, rows), jnp.float32),
             pltpu.VMEM((reps, 8, rows), jnp.float32),
             dma((2, reps)), dma((experts,)), dma((experts,)), dma((3, experts)), dma((3, experts)),
-            dma((chunks,)), dma((chunks,)), dma((chunks,)), dma((chunks,)),
+            dma((chunks, 2)), dma((chunks, 2)), dma((chunks,)), dma((chunks,)),
             dma((experts,)), dma((experts,)), dma((reps,)), dma((reps,)),
         ],
         compiler_params=pltpu.CompilerParams(

time: 56.3 us -> 56.5 us (level)
  no operation moved by 1% of the time
where the time goes in v2:
time: 56.5 us; the launch traced here: 56.3 us
  Pallas kernels  51.4 us (91%)
  local copies, waits for them, and re-layouts  4.17 us (7%)
  between operations  0.64 us (1%)
    pallas_call x1, Pallas kernels, per_device(): pl.pallas_call(kernel, out_shape=(jax.ShapeDtypeStruct((rows, quarter), h...  51.4 us
    unnamed x3, local copies, waits for them, and re-layouts  4.17 us

profile of v2, /device:TPU:0, one launch (start us, length us, event | category | flops | bytes accessed | tf_op | source)
XLA Modules:
  0.0 56.3 jit_solution(16384693329081638036)
XLA Ops:
  0.6 51.4 %shard_map.85 = (bf16[128,256]{1,0:T(8,128)(2,1)}, bf16[128,256]{1,0:T(8,128)(2,1)}, f32[2,128]{1,0:T(2,128)}) custom-call(s32[2,128]{1,0:T(2,128)} %bitcast.8, f32[2,128]{1,0:T(2,128)} %bitcast.9, bf16[128,256]{1,0:T(8,128)(2,1)} %tokens.1, bf16[128,256]{1,0:T(8,128)(2,1)} %cotangent.1, bf16[1024,1024]{1,0:T(8,128)(2,1)} %bitcast.5, bf16[1024,1024]{1,0:T(8,128)(2,1)} %bitcast.6), custom_call_target="tpu_custom_call" | custom-call | tf_op jit(solution)/shard_map/pallas_call | solution.py:406
  52.1 1.5 %copy.12 = bf16[128,256]{1,0:T(8,128)(2,1)} copy(bf16[128,256]{1,0:T(8,128)(2,1)} %get-tuple-element.12) | data formatting | bytes 131072
  53.6 1.5 %copy.13 = bf16[128,256]{1,0:T(8,128)(2,1)} copy(bf16[128,256]{1,0:T(8,128)(2,1)} %get-tuple-element.13) | data formatting | bytes 131072
  55.0 1.2 %copy.14 = f32[128,2]{0,1:T(2,128)} copy(f32[128,2]{0,1:T(2,128)} %bitcast.7) | data formatting | bytes 2048
